TPU v7x, 512 devices: a whole 4x4x16 slice. The times are simulated.
512 devices in a mesh: seq: 64 (over x, z), head: 8 (over y, core).
Axes of the slice: x: 4, y: 4, z: 16, core: 2. Of those that a mesh axis runs over, the one named last changes fastest.
Arguments:
- queries: bfloat16 [8192, 16, 128], P('seq', 'head'), may hold values from -21 to 21
- seq_keys: bfloat16 [8192, 16, 128], P('seq', 'head'), may hold values from -6 to 6
- seq_values: bfloat16 [8192, 16, 128], P('seq', 'head'), may hold values from -24 to 24
- memory_keys: bfloat16 [8192, 16, 128], P('seq', 'head'), may hold values from -6 to 6
- memory_values: bfloat16 [8192, 16, 128], P('seq', 'head'), may hold values from -24 to 24
- retrieval: int32 [64, 8], P('seq'), may hold values from 0 to 63, all different within a row
- fifo_head: int32 [1], replicated, may hold values from 0 to 63
- head_gate: float32 [16], P('head'), may hold values from -2 to 2
- norm_gain: float32 [16, 128], P('head'), may hold values from 0.1 to 1.9
Outputs:
- attended: bfloat16 [8192, 16, 128], P('seq', 'head')
Inputs may be any that keep to these rules, and one draw needn't show every extreme that they name: `retrieval`: each row names 8 different memory blocks.
All inputs are finite; a program needn't handle non-finite values.
Results may differ from a plain program's by a relative error of at most 0.029.
Values may be sent and summed in bfloat16 or wider, within the bound.
No kernel may reach another device: no remote copies, remote signals or barrier semaphores. Data moves between devices by JAX's collectives and lax.ppermute only.
A program may use at most 128 MiB of HBM per device.

v0:
```python
import jax
import jax.numpy as jnp
from jax import lax
from jax.sharding import PartitionSpec as P

HEADS = 16
DH = 128
MBLK = 128
EXPIRED = 4
MASKED = -1e30


def fold_piece(softmax_state, query_rows, key_rows, value_rows, key_mask):
    old_max, old_sum, old_acc = softmax_state
    scores = jnp.einsum(
        "thd,shd->hts", query_rows, key_rows, preferred_element_type=jnp.float32
    ) * query_rows.shape[2] ** (-0.5)
    scores = jnp.where(key_mask[None], scores, MASKED)
    row_max = jnp.maximum(old_max, jnp.max(scores, -1))
    exp_scores = jnp.where(key_mask[None], jnp.exp(scores - row_max[:, :, None]), 0.0)
    new_sum = jnp.sum(exp_scores, -1)
    new_acc = jnp.einsum(
        "hts,shd->htd",
        exp_scores.astype(jnp.bfloat16),
        value_rows,
        preferred_element_type=jnp.float32,
    )
    return (row_max, new_sum, new_acc)


def on_device(
    queries,
    seq_keys,
    seq_values,
    memory_keys,
    memory_values,
    retrieval,
    fifo_head,
    head_gate,
    norm_gain,
):
    tok_rows, head_count, head_width = queries.shape
    seq_devices = lax.axis_size("seq")
    my_index = lax.axis_index("seq")
    block_count = seq_devices * tok_rows // MBLK
    query_pos = my_index * tok_rows + jnp.arange(tok_rows, dtype=jnp.int32)
    wanted = retrieval[0]
    head_pos = fifo_head[0]

    def fresh_state():
        return (
            jnp.full((head_count, tok_rows), MASKED, jnp.float32),
            jnp.zeros((head_count, tok_rows), jnp.float32),
            jnp.zeros((head_count, tok_rows, head_width), jnp.float32),
        )

    pieces = (
        lax.all_gather(seq_keys, "seq", axis=0, tiled=True),
        lax.all_gather(seq_values, "seq", axis=0, tiled=True),
    )
    key_pos = jnp.arange(pieces[0].shape[0], dtype=jnp.int32)
    local_state = fold_piece(
        fresh_state(), queries, pieces[0], pieces[1], key_pos[None, :] <= query_pos[:, None]
    )
    pieces = (
        lax.all_gather(memory_keys, "seq", axis=0, tiled=True),
        lax.all_gather(memory_values, "seq", axis=0, tiled=True),
    )
    row_count = pieces[0].shape[0]
    block_ids = jnp.arange(row_count, dtype=jnp.int32) // MBLK
    is_live = jnp.mod(block_ids - head_pos + block_count, block_count) >= EXPIRED
    block_ids, is_live = (block_ids, is_live)
    chosen = jnp.any(block_ids[:, None] == wanted[None, :], -1) & is_live
    memory_state = fold_piece(
        fresh_state(),
        queries,
        pieces[0],
        pieces[1],
        jnp.broadcast_to(chosen[None, :], (tok_rows, row_count)),
    )
    local_out = local_state[2] / local_state[1][:, :, None]
    memory_out = memory_state[2] / memory_state[1][:, :, None]
    gate_mix = jax.nn.sigmoid(head_gate)[:, None, None]
    combined = gate_mix * memory_out + (1.0 - gate_mix) * local_out
    squares = lax.psum(jnp.sum(combined * combined, axis=(0, 2)), "head")
    row_scale = lax.rsqrt(squares / (HEADS * DH) + 1e-06)
    result = combined * row_scale[None, :, None] * norm_gain[:, None, :]
    return jnp.transpose(result, (1, 0, 2)).astype(jnp.bfloat16)


def solution(mesh):
    in_specs = (
        P("seq", "head", None),
        P("seq", "head", None),
        P("seq", "head", None),
        P("seq", "head", None),
        P("seq", "head", None),
        P("seq", None),
        P(),
        P("head"),
        P("head", None),
    )
    out_specs = P("seq", "head", None)
    return jax.shard_map(
        on_device, mesh=mesh, in_specs=in_specs, out_specs=out_specs, check_vma=False
    )
```

profile of v0, /device:TPU:1, one launch (start us, length us, event | category | flops | bytes accessed | tf_op | source)
XLA Modules:
  0.0 618.5 jit_solution(12764481445013468850)
XLA Ops:
  6.5 0.0 all-gather.5.cloned.1.call-start
  6.5 1.5 copy.17
  8.0 0.0 all-gather.5.cloned.1.call-update
  8.1 0.0 all-gather.9.cloned.1.call-start
  8.1 1.5 copy.20
  9.6 0.0 all-gather.9.cloned.1.call-update
  9.6 0.0 all-gather.7.cloned.1.call-start
  9.7 1.6 copy.19
  11.2 0.0 all-gather.7.cloned.1.call-update
  11.3 0.0 all-gather.11.cloned.1.call-start
  11.3 1.6 copy.22
  12.9 0.0 all-gather.11.cloned.1.call-update
  13.6 0.8 compare_reduce_fusion
  14.4 0.7 broadcast_subtract_fusion
  15.1 0.7 iota_compare_fusion
  15.8 138.3 %all-gather.5.cloned.1.call-done = bf16[8192,2,128]{2,0,1:T(8,128)(2,1)} async-done(((bf16[128,2,128]{2,0,1:T(8,128)(2,1)}), bf16[8192,2,128]{2,0,1:T(8,128)(2,1)}) %all-gather.5.cloned.1.call-update) | async-done | bytes 4194320 | tf_op jit(solution)/shard_map/all_gather | solution.py:66
  154.1 6.8 %fusion.33 = (f32[2,128]{1,0:T(2,128)S(1)}, f32[2,128,8192]{2,1,0:T(8,128)}) fusion(bf16[8192,2,128]{2,0,1:T(8,128)(2,1)} %all-gather.5.cloned.1.call-done, bf16[128,2,128]{2,1,0:T(2,128)(2,1)} %param.9, pred[8192]{0:T(1024)(128)(4,1)S(1)} %fusion.29), kind=kOutput, calls=%fused_computation.53 | convolution fusion | flops 543162112 | bytes 12657664 | tf_op jit(solution)/shard_map/thd,shd->hts/dot_general | solution.py:15
  160.9 137.4 %all-gather.9.cloned.1.call-done = bf16[8192,2,128]{2,0,1:T(8,128)(2,1)} async-done(((bf16[128,2,128]{2,0,1:T(8,128)(2,1)}), bf16[8192,2,128]{2,0,1:T(8,128)(2,1)}) %all-gather.9.cloned.1.call-update) | async-done | bytes 4194320 | tf_op jit(solution)/shard_map/all_gather | solution.py:58
  298.3 0.0 copy-done.2
  298.3 4.5 fusion.32
  302.8 0.1 copy-done.1
  303.0 1.8 fusion.2
  304.8 1.3 copy-done
  306.0 2.1 fusion.4
  308.2 132.3 %all-gather.7.cloned.1.call-done = bf16[8192,2,128]{0,2,1:T(8,128)(2,1)} async-done(((bf16[128,2,128]{0,2,1:T(8,128)(2,1)}), bf16[8192,2,128]{0,2,1:T(8,128)(2,1)}) %all-gather.7.cloned.1.call-update) | async-done | bytes 4194320 | tf_op jit(solution)/shard_map/all_gather | solution.py:67
  440.5 6.0 fusion.8
  446.5 136.7 %all-gather.11.cloned.1.call-done = bf16[8192,2,128]{0,2,1:T(8,128)(2,1)} async-done(((bf16[128,2,128]{0,2,1:T(8,128)(2,1)}), bf16[8192,2,128]{0,2,1:T(8,128)(2,1)}) %all-gather.11.cloned.1.call-update) | async-done | bytes 4194320 | tf_op jit(solution)/shard_map/all_gather | solution.py:59
  583.2 6.3 %multiply_reduce_fusion = (f32[128]{0:T(128)S(1)}, f32[2,128,128]{1,2,0:T(8,128)S(1)}) fusion(f32[2,128,128]{1,2,0:T(8,128)S(1)} %fusion.8, f32[2,128]{1,0:T(2,128)S(1)} %fusion.4, f32[2]{0:T(128)S(1)} %get-tuple-element.5, f32[2,128]{1,0:T(2,128)S(1)} %fusion.2, f32[2]{0:T(128)S(1)} %get-tuple-element.6, ...), kind=kOutput, calls=%fused_computation.27 | convolution fusion | flops 543391616 | bytes 13897232 | tf_op jit(solution)/shard_map/hts,shd->htd/dot_general | solution.py:22
  589.5 21.6 %psum.7 = f32[128]{0:T(128)S(1)} all-reduce(f32[128]{0:T(128)S(1)} %get-tuple-element.11), channel_id=1, replica_groups=mesh['seq'=64,'head'=8] {'head'}, use_global_device_ids=true, to_apply=%region_6.7 | all-reduce | flops 128 | bytes 1024 | tf_op jit(solution)/shard_map/psum | solution.py:85
  611.1 0.0 copy-done.3
  611.1 0.1 fusion.21
  611.2 0.8 copy.23
  (10 shorter events, 0.1 us)
Async XLA Ops:
  6.5 291.8 %copy-start.2 = (bf16[128,2,128]{2,1,0:T(2,128)(2,1)S(1)}, bf16[128,2,128]{2,1,0:T(2,128)(2,1)}, u32[]{:S(2)}) copy-start(bf16[128,2,128]{2,1,0:T(2,128)(2,1)} %param.9) | copy-start | bytes 196612
  6.5 147.6 %all-gather.5.cloned.1.call-start = ((), (), s32[]{:S(2)}) async-start(), calls=%async_computation | async-start | bytes 4259840 | tf_op jit(solution)/shard_map/all_gather | solution.py:66
  8.1 290.3 %all-gather.9.cloned.1.call-start = ((), (), s32[]{:S(2)}) async-start(), calls=%async_computation.2 | async-start | bytes 4259840 | tf_op jit(solution)/shard_map/all_gather | solution.py:58
  9.6 430.9 %all-gather.7.cloned.1.call-start = ((), (), s32[]{:S(2)}) async-start(), calls=%async_computation.1 | async-start | bytes 4259840 | tf_op jit(solution)/shard_map/all_gather | solution.py:67
  11.3 571.9 %all-gather.11.cloned.1.call-start = ((), (), s32[]{:S(2)}) async-start(), calls=%async_computation.3 | async-start | bytes 4259840 | tf_op jit(solution)/shard_map/all_gather | solution.py:59
  298.3 4.6 copy-start.1
  302.8 3.2 copy-start
  583.2 28.0 %copy-start.3 = (f32[2,128]{1,0:T(2,128)S(1)}, f32[2,128]{1,0:T(2,128)}, u32[]{:S(2)}) copy-start(f32[2,128]{1,0:T(2,128)} %param.17) | copy-start | bytes 3076
Sparse Core Ops, SparseCore 0:
  10.3 143.7 all-gather.4
  157.1 141.2 all-gather.8
  301.2 139.1 all-gather.6
  443.2 139.8 all-gather.10
where the time goes:
time: 619 us
  waiting for transfers between devices  545 us (88%)
  matrix products  23.6 us (4%)
  blocking collectives  21.6 us (3%)
  between operations  13.8 us (2%)
  local copies, waits for them, and re-layouts  8.29 us (1%)
  other arithmetic  6.25 us (1%)
    all_gather x1, waiting for transfers between devices, on_device(): lax.all_gather(memory_keys, 'seq', axis=0, tiled=True)  138 us
    all_gather x1, waiting for transfers between devices, on_device(): lax.all_gather(seq_keys, 'seq', axis=0, tiled=True)  137 us
    all_gather x1, waiting for transfers between devices, on_device(): lax.all_gather(seq_values, 'seq', axis=0, tiled=True)  137 us
    all_gather x1, waiting for transfers between devices, on_device(): lax.all_gather(memory_values, 'seq', axis=0, tiled=True)  132 us
    psum x1, blocking collectives, on_device(): squares = lax.psum(jnp.sum(combined * combined, axis=(0, 2)), 'head')  21.6 us
  transfers between devices with their start and end apart: 4, of which 4 were waited for; matrix products, arithmetic and copies ran while one was open for 5% of the time, Pallas kernels for 0%

commit v1 on v0

--- a/solution.py
+++ b/solution.py
@@ -55,7 +55,9 @@
         )
 
     pieces = (
-        lax.all_gather(seq_keys, "seq", axis=0, tiled=True),
+        jnp.concatenate(
+            lax.all_to_all(jnp.stack([seq_keys] * lax.axis_size("seq")), "seq", 0, 0), axis=0
+        ),
         lax.all_gather(seq_values, "seq", axis=0, tiled=True),
     )
     key_pos = jnp.arange(pieces[0].shape[0], dtype=jnp.int32)

time: 619 us -> 563 us (0.910)
  waiting for transfers between devices: 545 us -> 468 us
  starting transfers between devices: 0.13 us -> 19.5 us
  local copies, waits for them, and re-layouts: 8.29 us -> 16.8 us
    all_gather x1 -> x0, waiting for transfers between devices: 137 us -> none  [on_device(): lax.all_gather(seq_keys, 'seq', axis=0, tiled=True)]
    all_gather x1, waiting for transfers between devices: 138 us -> 210 us  [on_device(): lax.all_gather(memory_keys, 'seq', axis=0, tiled=True)]
    all_to_all x0 -> x1, starting transfers between devices: none -> 19.4 us  [on_device(): lax.all_to_all(jnp.stack([seq_keys] * lax.axis_size('seq')), 'seq', 0, 0)]
    all_gather x1, waiting for transfers between devices: 137 us -> 127 us  [on_device(): lax.all_gather(seq_values, 'seq', axis=0, tiled=True)]
  transfers between devices with their start and end apart: 4 -> 4, of which waited for: 4 -> 3; matrix products, arithmetic and copies ran while one was open for 5% -> 4% of each run, Pallas kernels for 0% -> 0%
where the time goes in v1:
time: 563 us
  waiting for transfers between devices  468 us (83%)
  blocking collectives  21.6 us (4%)
  starting transfers between devices  19.5 us (3%)
  matrix products  18.1 us (3%)
  local copies, waits for them, and re-layouts  16.8 us (3%)
  between operations  13.9 us (2%)
    all_gather x1, waiting for transfers between devices, on_device(): lax.all_gather(memory_keys, 'seq', axis=0, tiled=True)  210 us
    all_gather x1, waiting for transfers between devices, on_device(): lax.all_gather(memory_values, 'seq', axis=0, tiled=True)  132 us
    all_gather x1, waiting for transfers between devices, on_device(): lax.all_gather(seq_values, 'seq', axis=0, tiled=True)  127 us
    psum x1, blocking collectives, on_device(): squares = lax.psum(jnp.sum(combined * combined, axis=(0, 2)), 'head')  21.6 us
    all_to_all x1, starting transfers between devices, on_device(): lax.all_to_all(jnp.stack([seq_keys] * lax.axis_size('seq')), 'seq', 0, 0)  19.4 us
    dot_general x2, matrix products, fold_piece(): jnp.einsum('hts,shd->htd', exp_scores.astype(jnp.bfloat16), value_rows, p...  12.3 us
  transfers between devices with their start and end apart: 4, of which 3 were waited for; matrix products, arithmetic and copies ran while one was open for 4% of the time, Pallas kernels for 0%

profile of v1, /device:TPU:1, one launch (start us, length us, event | category | flops | bytes accessed | tf_op | source)
XLA Modules:
  0.0 562.9 jit_solution(11009289937705777814)
XLA Ops:
  6.5 0.0 all-gather.4.cloned.1.call-start
  6.6 1.5 copy.25
  8.1 0.0 all-gather.4.cloned.1.call-update
  8.1 0.9 copy.28
  9.0 3.0 stack.2
  12.0 19.4 %all-to-all-start = ((bf16[64,128,2,128]{3,1,2,0:T(8,128)(2,1)}), bf16[64,128,2,128]{3,1,2,0:T(8,128)(2,1)}, u32[]{:S(2)}, u32[]{:S(2)}) async-start(bf16[64,128,2,128]{3,1,2,0:T(8,128)(2,1)} %stack.2), calls=%async_computation | async-start | bytes 8388608 | tf_op jit(solution)/shard_map/all_to_all | solution.py:59
  31.4 0.0 all-gather.6.cloned.1.call-start
  31.4 0.7 copy.27
  32.2 0.0 all-gather.6.cloned.1.call-update
  32.2 0.0 all-gather.8.cloned.1.call-start
  32.2 0.0 copy-done.4
  32.3 0.8 copy.31
  33.0 0.0 all-gather.8.cloned.1.call-update
  33.7 0.2 compare_reduce_fusion
  33.9 0.7 iota_compare_fusion
  34.6 209.6 %all-gather.4.cloned.1.call-done = bf16[8192,2,128]{2,0,1:T(8,128)(2,1)} async-done(((bf16[128,2,128]{2,0,1:T(8,128)(2,1)}), bf16[8192,2,128]{2,0,1:T(8,128)(2,1)}) %all-gather.4.cloned.1.call-update) | async-done | bytes 4194320 | tf_op jit(solution)/shard_map/all_gather | solution.py:68
  244.2 3.6 fusion.33
  247.9 3.2 copy-done.1
  251.1 1.8 fusion.2
  252.9 131.8 %all-gather.6.cloned.1.call-done = bf16[8192,2,128]{0,2,1:T(8,128)(2,1)} async-done(((bf16[128,2,128]{0,2,1:T(8,128)(2,1)}), bf16[8192,2,128]{0,2,1:T(8,128)(2,1)}) %all-gather.6.cloned.1.call-update) | async-done | bytes 4194320 | tf_op jit(solution)/shard_map/all_gather | solution.py:69
  384.7 6.0 %fusion.8 = f32[2,128,128]{1,2,0:T(8,128)S(1)} fusion(bf16[8192,2,128]{0,2,1:T(8,128)(2,1)} %all-gather.6.cloned.1.call-done, f32[2,128,8192]{2,1,0:T(8,128)} %copy-done.1, f32[2,128]{1,0:T(2,128)S(1)} %broadcast_maximum_fusion.1, pred[8192]{0:T(1024)(128)(4,1)S(1)} %fusion.29), kind=kOutput, calls=%fused_computation.11 | convolution fusion | flops 543162368 | bytes 12723200 | tf_op jit(solution)/shard_map/hts,shd->htd/dot_general | solution.py:22
  390.7 0.0 all-to-all-done
  390.7 2.7 copy.29
  393.4 2.2 fusion.32
  395.7 3.2 copy-done
  398.9 2.1 fusion.4
  401.0 126.5 %all-gather.8.cloned.1.call-done = bf16[8192,2,128]{0,2,1:T(8,128)(2,1)} async-done(((bf16[128,2,128]{0,2,1:T(8,128)(2,1)}), bf16[8192,2,128]{0,2,1:T(8,128)(2,1)}) %all-gather.8.cloned.1.call-update) | async-done | bytes 4194320 | tf_op jit(solution)/shard_map/all_gather | solution.py:61
  527.5 6.3 %multiply_reduce_fusion = (f32[128]{0:T(128)S(1)}, f32[2,128,128]{1,2,0:T(8,128)S(1)}) fusion(f32[2,128,128]{1,2,0:T(8,128)S(1)} %fusion.8, f32[2,128]{1,0:T(2,128)S(1)} %fusion.4, f32[2]{0:T(128)S(1)} %get-tuple-element.5, f32[2,128]{1,0:T(2,128)S(1)} %fusion.2, f32[2]{0:T(128)S(1)} %get-tuple-element.6, ...), kind=kOutput, calls=%fused_computation.27 | convolution fusion | flops 543391616 | bytes 13897232 | tf_op jit(solution)/shard_map/hts,shd->htd/dot_general | solution.py:22
  533.8 21.6 %psum.7 = f32[128]{0:T(128)S(1)} all-reduce(f32[128]{0:T(128)S(1)} %get-tuple-element.11), channel_id=1, replica_groups=mesh['seq'=64,'head'=8] {'head'}, use_global_device_ids=true, to_apply=%region_6.7 | all-reduce | flops 128 | bytes 1024 | tf_op jit(solution)/shard_map/psum | solution.py:87
  555.5 0.0 copy-done.5
  555.5 0.1 fusion.21
  555.6 0.8 copy.32
  (19 shorter events, 0.1 us)
Async XLA Ops:
  6.5 24.9 %copy-start.3 = (bf16[128,2,128]{2,1,0:T(2,128)(2,1)S(1)}, bf16[128,2,128]{2,1,0:T(2,128)(2,1)}, u32[]{:S(2)}) copy-start(bf16[128,2,128]{2,1,0:T(2,128)(2,1)} %param.13) | copy-start | bytes 196612
  6.5 25.7 %copy-start.4 = (bf16[128,2,128]{2,1,0:T(2,128)(2,1)S(1)}, bf16[128,2,128]{2,1,0:T(2,128)(2,1)}, u32[]{:S(2)}) copy-start(bf16[128,2,128]{2,1,0:T(2,128)(2,1)} %param.11) | copy-start | bytes 196612
  6.5 27.2 %copy-start.6 = (s32[1,8]{1,0:T(1,128)S(1)}, s32[1,8]{1,0:T(1,128)}, u32[]{:S(2)}) copy-start(s32[1,8]{1,0:T(1,128)} %param.14) | copy-start | bytes 100
  6.5 27.3 %copy-start.7 = (f32[2]{0:T(128)S(1)}, f32[2]{0:T(128)}, u32[]{:S(2)}) copy-start(f32[2]{0:T(128)} %param.16) | copy-start | bytes 28
  6.5 237.7 %copy-start.2 = (bf16[128,2,128]{2,1,0:T(2,128)(2,1)S(1)}, bf16[128,2,128]{2,1,0:T(2,128)(2,1)}, u32[]{:S(2)}) copy-start(bf16[128,2,128]{2,1,0:T(2,128)(2,1)} %param.9) | copy-start | bytes 196612
  6.5 237.7 %all-gather.4.cloned.1.call-start = ((), (), s32[]{:S(2)}) async-start(), calls=%async_computation.1 | async-start | bytes 4259840 | tf_op jit(solution)/shard_map/all_gather | solution.py:68
  12.0 378.7 %all-to-all-start = ((bf16[64,128,2,128]{3,1,2,0:T(8,128)(2,1)}), bf16[64,128,2,128]{3,1,2,0:T(8,128)(2,1)}, u32[]{:S(2)}, u32[]{:S(2)}) async-start(bf16[64,128,2,128]{3,1,2,0:T(8,128)(2,1)} %stack.2), calls=%async_computation | async-start | bytes 8388608 | tf_op jit(solution)/shard_map/all_to_all | solution.py:59
  31.4 353.3 %all-gather.6.cloned.1.call-start = ((), (), s32[]{:S(2)}) async-start(), calls=%async_computation.2 | async-start | bytes 4259840 | tf_op jit(solution)/shard_map/all_gather | solution.py:69
  32.2 495.3 %all-gather.8.cloned.1.call-start = ((), (), s32[]{:S(2)}) async-start(), calls=%async_computation.3 | async-start | bytes 4259840 | tf_op jit(solution)/shard_map/all_gather | solution.py:61
  247.8 3.2 copy-start.1
  395.7 3.2 copy-start
  527.5 28.0 %copy-start.5 = (f32[2,128]{1,0:T(2,128)S(1)}, f32[2,128]{1,0:T(2,128)}, u32[]{:S(2)}) copy-start(f32[2,128]{1,0:T(2,128)} %param.17) | copy-start | bytes 3076
Sparse Core Ops, SparseCore 0:
  10.3 233.8 all-gather.3
  247.1 137.5 all-gather.5
  387.6 139.8 all-gather.7
